TPU v7x, 256 devices: a whole 4x4x8 slice. The times are simulated.
256 devices in a mesh: space: 64 (over z, x_hi, y), freq: 4 (over x_lo, core).
Axes of the slice: x: 4 (x_hi: 2, x_lo: 2; x = x_hi * 2 + x_lo), y: 4, z: 8, core: 2. Of those that a mesh axis runs over, the one named last changes fastest.
Arguments:
- forcing: bfloat16 [4, 32, 8, 64, 1536], P(None, 'freq', None, 'space'), may hold values from -36 to 36
- base_harm: float32 [7, 2, 64, 1536], P(None, None, 'space'), may hold values from -6 to 6
- mixing: float32 [7, 4, 4], replicated, may hold values from -3 to 3
- mean_flow: float32 [1536], replicated, may hold values from 0.2 to 1.2
- harm_lo: int32 [1], replicated, may hold values from -20 to -9
- couple_flags: int32 [32, 7], P('freq'), may hold values 0 or 1
Outputs:
- response: bfloat16 [4, 32, 8, 64, 1536], P(None, 'freq', None, 'space')
- gram_matrix: float32 [4, 4], replicated
All inputs are finite; a program needn't handle non-finite values. No bound on the sum of `couple_flags` on one device may be relied on, other than what follows from the above.
Results may differ from a plain program's by a relative error of at most 0.004.
Values may be sent and summed in bfloat16 or wider, within the bound.
A program may use at most 128 MiB of HBM per device.

v0:
```python
import jax
import jax.numpy as jnp
from jax import lax
from jax.sharding import PartitionSpec as P

V = 4
NY = 32
NZ = 48


OMEGA = 0.05
VISCOSITY = 0.25


def passed_along(value, axis, by):
    devices = lax.axis_size(axis)
    pairs = [(i, i + by) for i in range(devices) if 0 <= i + by < devices]
    return lax.ppermute(value, axis, pairs)


def with_halo(cells, sides, width):
    for axis, dim in sides:
        count = lax.axis_size(axis)
        ends = count - 1
        head = lax.slice_in_dim(cells, 0, width, axis=dim)
        tail = lax.slice_in_dim(cells, cells.shape[dim] - width, cells.shape[dim], axis=dim)
        cells = jnp.concatenate(
            [
                lax.ppermute(tail, axis, [(i, (i + 1) % count) for i in range(ends)]),
                cells,
                lax.ppermute(head, axis, [((i + 1) % count, i) for i in range(ends)]),
            ],
            axis=dim,
        )
    return cells


def copy_for_each(value, axis):
    copies = jnp.broadcast_to(value, (lax.axis_size(axis), *value.shape))
    return lax.all_to_all(copies, axis, split_axis=0, concat_axis=0, tiled=True)


def of_everyone(value, axis):
    everything = copy_for_each(value, axis)
    return jnp.sum(everything, axis=0)


def crossflow(values):
    cells = NY * NZ
    position = jnp.arange(cells, dtype=jnp.int32)
    span_pos = position % NZ
    wake_pos = position // NZ
    span_up = jnp.where(span_pos == NZ - 1, jnp.roll(values, NZ - 1, -1), jnp.roll(values, -1, -1))
    span_down = jnp.where(span_pos == 0, jnp.roll(values, 1 - NZ, -1), jnp.roll(values, 1, -1))
    wake_up = jnp.where(wake_pos == NY - 1, 0.0, jnp.roll(values, -NZ, -1))
    wake_down = jnp.where(wake_pos == 0, 0.0, jnp.roll(values, NZ, -1))
    return VISCOSITY * (wake_up + wake_down + span_up + span_down - 6.0 * values)


def streamwise(left_vals, right_vals, stream):
    return (VISCOSITY + 0.5 * stream) * left_vals + (VISCOSITY - 0.5 * stream) * right_vals


def rotation(values, frequency):
    spin_rate = (OMEGA * frequency)[:, None, None, None]
    real_part = values[..., :V, :, :]
    imag_part = values[..., V:, :, :]
    return jnp.concatenate([-spin_rate * imag_part, spin_rate * real_part], axis=-3)


def coupling(padded, base_modes, mixing, couplers):
    count_h = couplers.shape[0]
    summed = None
    for j in range(7):
        offset = j - 3
        source = lax.slice_in_dim(padded, 3 - offset, 3 - offset + count_h, axis=padded.ndim - 4)
        halves = source.reshape(source.shape[:-3] + (2, V) + source.shape[-2:])
        blended = jnp.einsum(
            "vw,...cwxn->...cvxn", mixing[j], halves, precision=lax.Precision.HIGHEST
        )
        base_re = base_modes[j, 0]
        base_im = base_modes[j, 1]
        mix_re = blended[..., 0, :, :, :]
        mix_im = blended[..., 1, :, :, :]
        product_term = jnp.stack(
            [base_re * mix_re - base_im * mix_im, base_re * mix_im + base_im * mix_re], axis=-4
        )
        weights = couplers[:, j].astype(jnp.float32)[:, None, None, None, None]
        contrib = weights * product_term
        summed = contrib if summed is None else summed + contrib
    return summed.reshape(summed.shape[:-5] + (count_h, 2 * V) + summed.shape[-2:])


def local(forcing, base_harm, mixing, mean_flow, harm_lo, couple_flags):
    count_h = forcing.shape[1]
    planes = forcing.shape[3]
    widened = forcing.astype(jnp.float32)
    zero_plane = jnp.zeros_like(widened)
    left_vals = jnp.concatenate([zero_plane, widened[:, :, :, :-1, :]], axis=3)
    right_vals = jnp.concatenate([widened[:, :, :, 1:, :], zero_plane], axis=3)
    interior = streamwise(left_vals, right_vals, mean_flow)
    going_right = (VISCOSITY + 0.5 * mean_flow) * widened
    going_left = (VISCOSITY - 0.5 * mean_flow) * widened
    from_left = passed_along(going_right.astype(jnp.bfloat16), "space", 1).astype(going_right.dtype)
    from_right = passed_along(going_left.astype(jnp.bfloat16), "space", -1).astype(going_left.dtype)
    along_x = interior + from_left + from_right
    spatial = crossflow(widened) + along_x
    rim_block = with_halo(forcing, (("freq", 1),), 3)
    padded = rim_block.astype(jnp.float32)
    start_k = lax.axis_index("freq") * count_h
    frequency = (harm_lo[0] + start_k + jnp.arange(count_h, dtype=jnp.int32)).astype(jnp.float32)
    result = (
        rotation(widened, frequency) - spatial - coupling(padded, base_harm, mixing, couple_flags)
    )
    response = result.astype(jnp.bfloat16)
    flattened = response.reshape(response.shape[0], -1)
    cells_all = (
        count_h
        * lax.axis_size("freq")
        * forcing.shape[2]
        * planes
        * lax.axis_size("space")
        * forcing.shape[4]
    )
    partial_value = jnp.dot(flattened, flattened.T, preferred_element_type=jnp.float32) / cells_all
    gram_matrix = of_everyone(partial_value, "space")
    gram_matrix = of_everyone(gram_matrix, "freq")
    return (response, gram_matrix)


def solution(mesh):
    return jax.shard_map(
        local,
        mesh=mesh,
        in_specs=(
            P(None, "freq", None, "space", None),
            P(None, None, "space", None),
            P(),
            P(),
            P(),
            P("freq", None),
        ),
        out_specs=(P(None, "freq", None, "space", None), P()),
        check_vma=False,
    )
```

profile of v0, /device:TPU:1, one launch (start us, length us, event | category | flops | bytes accessed | tf_op | source)
XLA Modules:
  0.0 127.6 jit_solution(1238740218257295337)
XLA Ops:
  1.8 5.1 %collective-permute-start.2 = (bf16[4,3,8,1,1536]{4,2,3,1,0:T(8,128)(2,1)S(1)}, bf16[4,3,8,1,1536]{4,2,3,1,0:T(8,128)(2,1)S(1)}, u32[]{:S(2)}, u32[]{:S(2)}) collective-permute-start(bf16[4,3,8,1,1536]{4,2,3,1,0:T(8,128)(2,1)S(1)} %get-tuple-element.54), channel_id=1, source_target_pairs={{1,0},{2,1},{3,2},{5,4},{6,5},{7,6},{9,8},{10,9},{11,10},{13,12},{... | collective-permute-start | bytes 884744 | tf_op jit(solution)/shard_map/ppermute | solution.py:31
  7.0 1.9 %collective-permute-start.3 = (bf16[4,3,8,1,1536]{4,2,3,1,0:T(8,128)(2,1)S(1)}, bf16[4,3,8,1,1536]{4,2,3,1,0:T(8,128)(2,1)S(1)}, u32[]{:S(2)}, u32[]{:S(2)}) collective-permute-start(bf16[4,3,8,1,1536]{4,2,3,1,0:T(8,128)(2,1)S(1)} %get-tuple-element.55), channel_id=1, source_target_pairs={{0,1},{1,2},{2,3},{4,5},{5,6},{6,7},{8,9},{9,10},{10,11},{12,13},{... | collective-permute-start | bytes 884744 | tf_op jit(solution)/shard_map/ppermute | solution.py:29
  11.6 3.5 %collective-permute-start = (bf16[4,8,8,1,1536]{4,2,3,1,0:T(8,128)(2,1)}, bf16[4,8,8,1,1536]{4,2,3,1,0:T(8,128)(2,1)}, u32[]{:S(2)}, u32[]{:S(2)}) collective-permute-start(bf16[4,8,8,1,1536]{4,2,3,1,0:T(8,128)(2,1)} %get-tuple-element.52), channel_id=1, source_target_pairs={{0,4},{4,8},{8,12},{12,16},{16,20},{20,24},{24,28},{28,32},{32,36}... | collective-permute-start | bytes 2359304 | tf_op jit(solution)/shard_map/ppermute | solution.py:18
  19.3 2.1 %fusion.38 = (f32[4,8,8,1,1489]{4,2,3,1,0:T(8,128)}, f32[4,8,8,1,1489]{4,2,3,1,0:T(8,128)}) fusion(bf16[4,8,8,1,1536]{4,2,3,1,0:T(8,128)(2,1)S(1)} %copy-done), kind=kLoop, calls=%fused_computation.125 | loop fusion | bytes 6098944 | tf_op jit(solution)/shard_map/jit(_roll_static)/slice | solution.py:54
  21.4 2.1 %fusion.41 = (f32[4,8,8,1,1488]{4,2,3,1,0:T(8,128)}, f32[4,8,8,1,1488]{4,2,3,1,0:T(8,128)}) fusion(bf16[4,8,8,1,1536]{4,2,3,1,0:T(8,128)(2,1)S(1)} %copy-done), kind=kLoop, calls=%fused_computation.128 | loop fusion | bytes 6094848 | tf_op jit(solution)/shard_map/jit(_roll_static)/slice | solution.py:56
  23.5 2.1 %fusion.37 = (f32[4,8,8,1,1535]{4,2,3,1,0:T(8,128)}, f32[4,8,8,1,1535]{4,2,3,1,0:T(8,128)}) fusion(bf16[4,8,8,1,1536]{4,2,3,1,0:T(8,128)(2,1)S(1)} %copy-done), kind=kLoop, calls=%fused_computation.124 | loop fusion | bytes 6287360 | tf_op jit(solution)/shard_map/jit(_roll_static)/slice | solution.py:54
  28.0 2.6 %convolution_bitcast_fusion.3 = f32[4,8,2,4,1,1536]{5,3,2,1,0,4:T(4,128)} fusion(bf16[4,8,2,4,1536]{4,3,2,1,0:T(4,128)(2,1)S(1)} %reshape.596, f32[4,4]{1,0:T(4,128)S(1)} %get-tuple-element.18), kind=kOutput, calls=%fused_computation.3 | convolution fusion | flops 18874368 | bytes 2359360 | tf_op jit(solution)/shard_map/vw,...cwxn->...cvxn/dot_general | solution.py:78
  35.0 2.1 %convolution_bitcast_fusion.6 = f32[4,8,2,4,1,1536]{5,3,2,1,0,4:T(4,128)S(1)} fusion(bf16[4,8,2,4,1536]{4,3,2,1,0:T(4,128)(2,1)S(1)} %reshape.593, f32[4,4]{1,0:T(4,128)} %get-tuple-element.16), kind=kOutput, calls=%fused_computation.6 | convolution fusion | flops 18874368 | bytes 2359360 | tf_op jit(solution)/shard_map/vw,...cwxn->...cvxn/dot_general | solution.py:78
  37.8 1.7 %stack.50 = f32[4,8,8,1,1536]{4,2,1,0,3:T(8,128)} reshape(f32[4,8,2,4,1,1536]{5,3,2,1,0,4:T(4,128)S(1)} %pad_maximum_fusion) | data formatting | bytes 3145728 | tf_op jit(solution)/shard_map/stack | solution.py:85
  39.5 1.8 %reshape.595 = bf16[4,8,2,4,1536]{4,3,2,1,0:T(4,128)(2,1)S(1)} reshape(bf16[4,8,8,1,1536]{4,2,3,1,0:T(8,128)(2,1)} %get-tuple-element.47) | data formatting | bytes 1572864 | tf_op jit(solution)/shard_map/reshape.29
  45.1 1.8 %multiply_subtract_fusion.4 = (f32[4,8,1,4,1,1536]{5,3,2,1,0,4:T(4,128)S(1)}, f32[4,8,1,4,1,1536]{5,3,2,1,0,4:T(4,128)S(1)}, f32[4,8,1,4,1,1536]{5,3,2,1,0,4:T(4,128)}, f32[4,8,1,4,1,1536]{5,3,2,1,0,4:T(4,128)}) fusion(f32[4,8,2,4,1,1536]{5,3,2,1,0,4:T(4,128)S(1)} %convolution_bitcast_fusion.4, f32[1536]{0:T(1024)S(1)} %get-tuple-element.9, ...), kind=kLoop, calls=%fused_computation.55 | loop fusion | flops 2359296 | bytes 6316032 | tf_op jit(solution)/shard_map/sub | solution.py:86
  47.3 1.7 %stack.54 = f32[4,8,8,1,1536]{4,2,1,0,3:T(8,128)} reshape(f32[4,8,2,4,1,1536]{5,3,2,1,0,4:T(4,128)S(1)} %pad_maximum_fusion.2) | data formatting | bytes 3145728 | tf_op jit(solution)/shard_map/stack | solution.py:85
  49.0 1.8 %pad_maximum_fusion.1 = f32[4,8,2,4,1,1536]{5,3,2,1,0,4:T(4,128)S(1)} fusion(f32[4,8,1,4,1,1536]{5,3,2,1,0,4:T(4,128)} %get-tuple-element.80, f32[4,8,1,4,1,1536]{5,3,2,1,0,4:T(4,128)} %get-tuple-element.81), kind=kLoop, calls=%fused_computation.21 | loop fusion | flops 393216 | bytes 3145728 | tf_op jit(solution)/shard_map/stack | solution.py:85
  53.8 1.7 %reshape.597 = bf16[4,8,2,4,1536]{4,3,2,1,0:T(4,128)(2,1)S(1)} reshape(bf16[4,8,8,1,1536]{4,2,3,1,0:T(8,128)(2,1)} %get-tuple-element.49) | data formatting | bytes 1572864 | tf_op jit(solution)/shard_map/reshape.43
  56.9 1.9 %multiply_subtract_fusion.2 = (f32[4,8,1,4,1,1536]{5,3,2,1,0,4:T(4,128)S(1)}, f32[4,8,1,4,1,1536]{5,3,2,1,0,4:T(4,128)S(1)}, f32[4,8,1,4,1,1536]{5,3,2,1,0,4:T(4,128)}, f32[4,8,1,4,1,1536]{5,3,2,1,0,4:T(4,128)}) fusion(f32[4,8,2,4,1,1536]{5,3,2,1,0,4:T(4,128)S(1)} %convolution_bitcast_fusion.2, f32[1536]{0:T(1024)S(1)} %get-tuple-element.5, ...), kind=kLoop, calls=%fused_computation.51 | loop fusion | flops 2359296 | bytes 6316032 | tf_op jit(solution)/shard_map/sub | solution.py:86
  59.1 1.7 %stack.58 = f32[4,8,8,1,1536]{4,2,1,0,3:T(8,128)} reshape(f32[4,8,2,4,1,1536]{5,3,2,1,0,4:T(4,128)S(1)} %pad_maximum_fusion.4) | data formatting | bytes 3145728 | tf_op jit(solution)/shard_map/stack | solution.py:85
  60.8 1.9 %reshape.599 = bf16[4,8,2,4,1536]{4,3,2,1,0:T(4,128)(2,1)S(1)} reshape(bf16[4,8,8,1,1536]{4,2,3,1,0:T(8,128)(2,1)} %get-tuple-element.50) | data formatting | bytes 1572864 | tf_op jit(solution)/shard_map/reshape.57
  70.8 1.7 %stack.60 = f32[4,8,8,1,1536]{4,2,1,0,3:T(8,128)} reshape(f32[4,8,2,4,1,1536]{5,3,2,1,0,4:T(4,128)S(1)} %pad_maximum_fusion.5) | data formatting | bytes 3145728 | tf_op jit(solution)/shard_map/stack | solution.py:85
  74.1 1.7 %stack.56 = f32[4,8,8,1,1536]{4,2,1,0,3:T(8,128)} reshape(f32[4,8,2,4,1,1536]{5,3,2,1,0,4:T(4,128)S(1)} %pad_maximum_fusion.3) | data formatting | bytes 3145728 | tf_op jit(solution)/shard_map/stack | solution.py:85
  75.8 3.3 %slice_multiply_fusion.1 = (f32[4,8,4,1,1536]{4,2,3,1,0:T(4,128)S(1)}, f32[4,8,4,1,1536]{4,2,3,1,0:T(4,128)}) fusion(f32[4,8,8,1,1536]{4,2,3,1,0:T(8,128)} %get-tuple-element.57, f32[8]{0:T(128)} %get-tuple-element.75, f32[8]{0:T(128)} %get-tuple-element.74), kind=kLoop, calls=%fused_computation.45 | loop fusion | flops 393216 | bytes 3145792 | tf_op jit(solution)/shard_map/mul | solution.py:68
  79.2 11.0 %fusion.1 = bf16[4,8,8,1,1536]{4,2,3,1,0:T(8,128)(2,1)} fusion(f32[4,8,4,1,1536]{4,2,3,1,0:T(4,128)} %get-tuple-element.45, f32[4,8,4,1,1536]{4,2,3,1,0:T(4,128)S(1)} %get-tuple-element.44, f32[4,8,8,1,48]{4,2,3,1,0:T(8,128)} %get-tuple-element.68, f32[4,8,8,1,1488]{4,2,3,1,0:T(8,128)} %get-tuple-element.70, f32[4,8,8,1,1488]{4,2,3,1,0:T(8,128)} %get-tuple-element.69, ...), kind=kLoop, calls=%fused_computation.9 | loop fusion | flops 15335424 | bytes 25178336 | tf_op jit(solution)/shard_map/convert_element_type | solution.py:115
  90.2 3.0 %fusion.14 = f32[4,4]{1,0:T(4,128)S(1)} fusion(bf16[4,8,8,1536]{3,2,1,0:T(8,128)(2,1)} %bitcast.161), kind=kOutput, calls=%fused_computation.43 | convolution fusion | flops 3145744 | bytes 786496 | tf_op jit(solution)/shard_map/dot_general | solution.py:125
  93.3 26.2 %all_to_all.10 = f32[64,4,4]{2,1,0:T(4,128)S(1)} all-to-all(f32[64,4,4]{2,1,0:T(4,128)S(1)} %broadcast_in_dim.40), channel_id=1, replica_groups=mesh['space'=64,'freq'=4] {'space'}, dimensions={0} | all-to-all | bytes 8192 | tf_op jit(solution)/shard_map/all_to_all | solution.py:40
  119.6 7.4 %all_to_all.11 = f32[4,4,4]{2,1,0:T(4,128)S(1)} all-to-all(f32[4,4,4]{2,1,0:T(4,128)S(1)} %broadcast_in_dim.41), channel_id=1, replica_groups=mesh['space'=64,'freq'=4] {'freq'}, dimensions={0} | all-to-all | bytes 512 | tf_op jit(solution)/shard_map/all_to_all | solution.py:40
  (85 shorter events, 34.2 us)
Async XLA Ops:
  0.6 9.6 %copy-start = (bf16[4,8,8,1,1536]{4,2,3,1,0:T(8,128)(2,1)S(1)}, bf16[4,8,8,1,1536]{4,2,3,1,0:T(8,128)(2,1)}, u32[]{:S(2)}) copy-start(bf16[4,8,8,1,1536]{4,2,3,1,0:T(8,128)(2,1)} %param.6) | copy-start | bytes 2359300
  1.8 31.6 %collective-permute-start.2 = (bf16[4,3,8,1,1536]{4,2,3,1,0:T(8,128)(2,1)S(1)}, bf16[4,3,8,1,1536]{4,2,3,1,0:T(8,128)(2,1)S(1)}, u32[]{:S(2)}, u32[]{:S(2)}) collective-permute-start(bf16[4,3,8,1,1536]{4,2,3,1,0:T(8,128)(2,1)S(1)} %get-tuple-element.54), channel_id=1, source_target_pairs={{1,0},{2,1},{3,2},{5,4},{6,5},{7,6},{9,8},{10,9},{11,10},{13,12},{... | collective-permute-start | bytes 884744 | tf_op jit(solution)/shard_map/ppermute | solution.py:31
  7.0 25.0 %collective-permute-start.3 = (bf16[4,3,8,1,1536]{4,2,3,1,0:T(8,128)(2,1)S(1)}, bf16[4,3,8,1,1536]{4,2,3,1,0:T(8,128)(2,1)S(1)}, u32[]{:S(2)}, u32[]{:S(2)}) collective-permute-start(bf16[4,3,8,1,1536]{4,2,3,1,0:T(8,128)(2,1)S(1)} %get-tuple-element.55), channel_id=1, source_target_pairs={{0,1},{1,2},{2,3},{4,5},{5,6},{6,7},{8,9},{9,10},{10,11},{12,13},{... | collective-permute-start | bytes 884744 | tf_op jit(solution)/shard_map/ppermute | solution.py:29
  11.6 67.5 %collective-permute-start = (bf16[4,8,8,1,1536]{4,2,3,1,0:T(8,128)(2,1)}, bf16[4,8,8,1,1536]{4,2,3,1,0:T(8,128)(2,1)}, u32[]{:S(2)}, u32[]{:S(2)}) collective-permute-start(bf16[4,8,8,1,1536]{4,2,3,1,0:T(8,128)(2,1)} %get-tuple-element.52), channel_id=1, source_target_pairs={{0,4},{4,8},{8,12},{12,16},{16,20},{20,24},{24,28},{28,32},{32,36}... | collective-permute-start | bytes 2359304 | tf_op jit(solution)/shard_map/ppermute | solution.py:18
  15.1 64.1 %collective-permute-start.1 = (bf16[4,8,8,1,1536]{4,2,3,1,0:T(8,128)(2,1)}, bf16[4,8,8,1,1536]{4,2,3,1,0:T(8,128)(2,1)}, u32[]{:S(2)}, u32[]{:S(2)}) collective-permute-start(bf16[4,8,8,1,1536]{4,2,3,1,0:T(8,128)(2,1)} %get-tuple-element.53), channel_id=1, source_target_pairs={{4,0},{8,4},{12,8},{16,12},{20,16},{24,20},{28,24},{32,28},{36,32}... | collective-permute-start | bytes 2359304 | tf_op jit(solution)/shard_map/ppermute | solution.py:18
  23.5 2.8 %copy-start.10 = (s32[8,7]{1,0:T(8,128)S(1)}, s32[8,7]{1,0:T(8,128)}, u32[]{:S(2)}) copy-start(s32[8,7]{1,0:T(8,128)} %param.11) | copy-start | bytes 676
  23.5 3.6 %copy-start.9 = (f32[7,4,4]{0,2,1:T(4,128)S(1)}, f32[7,4,4]{0,2,1:T(4,128)}, u32[]{:S(2)}) copy-start(f32[7,4,4]{0,2,1:T(4,128)} %param.8) | copy-start | bytes 1348
  23.5 4.3 %copy-start.11 = (f32[7,2,1,1536]{3,2,1,0:T(1,128)S(1)}, f32[7,2,1,1536]{3,2,1,0:T(1,128)}, u32[]{:S(2)}) copy-start(f32[7,2,1,1536]{3,2,1,0:T(1,128)} %param.7) | copy-start | bytes 258052
  39.5 1.8 %copy-start.3 = (bf16[4,8,8,1,1536]{4,2,3,1,0:T(8,128)(2,1)S(1)}, bf16[4,8,8,1,1536]{4,2,3,1,0:T(8,128)(2,1)}, u32[]{:S(2)}) copy-start(bf16[4,8,8,1,1536]{4,2,3,1,0:T(8,128)(2,1)} %get-tuple-element.48) | copy-start | bytes 2359300
  39.5 2.8 %copy-start.17 = (f32[4,4]{1,0:T(4,128)S(1)}, f32[4,4]{1,0:T(4,128)}, u32[]{:S(2)}) copy-start(f32[4,4]{1,0:T(4,128)} %get-tuple-element.19) | copy-start | bytes 196
  42.3 1.4 %copy-start.5 = (bf16[4,8,2,4,1536]{4,3,2,1,0:T(4,128)(2,1)S(1)}, bf16[4,8,2,4,1536]{4,3,2,1,0:T(4,128)(2,1)}, u32[]{:S(2)}) copy-start(bf16[4,8,2,4,1536]{4,3,2,1,0:T(4,128)(2,1)} %reshape.594) | copy-start | bytes 2359300
  42.3 1.4 %copy-start.16 = (f32[4,4]{1,0:T(4,128)S(1)}, f32[4,4]{1,0:T(4,128)}, u32[]{:S(2)}) copy-start(f32[4,4]{1,0:T(4,128)} %get-tuple-element.20) | copy-start | bytes 196
  53.8 1.7 %copy-start.15 = (f32[4,4]{1,0:T(4,128)S(1)}, f32[4,4]{1,0:T(4,128)}, u32[]{:S(2)}) copy-start(f32[4,4]{1,0:T(4,128)} %get-tuple-element.17) | copy-start | bytes 196
  55.5 1.4 %copy-start.1 = (f32[4,8,2,4,1,1536]{5,3,2,1,0,4:T(4,128)S(1)}, f32[4,8,2,4,1,1536]{5,3,2,1,0,4:T(4,128)}, u32[]{:S(2)}) copy-start(f32[4,8,2,4,1,1536]{5,3,2,1,0,4:T(4,128)} %convolution_bitcast_fusion.3) | copy-start | bytes 4718596
  60.8 2.1 %copy-start.14 = (f32[4,4]{1,0:T(4,128)S(1)}, f32[4,4]{1,0:T(4,128)}, u32[]{:S(2)}) copy-start(f32[4,4]{1,0:T(4,128)} %get-tuple-element.21) | copy-start | bytes 196
  62.9 1.4 %copy-start.13 = (f32[4,4]{1,0:T(4,128)S(1)}, f32[4,4]{1,0:T(4,128)}, u32[]{:S(2)}) copy-start(f32[4,4]{1,0:T(4,128)} %get-tuple-element.22) | copy-start | bytes 196
  70.8 1.7 %copy-start.4 = (f32[4,8,1,4,1,1536]{5,3,2,1,0,4:T(4,128)S(1)}, f32[4,8,1,4,1,1536]{5,3,2,1,0,4:T(4,128)}, u32[]{:S(2)}) copy-start(f32[4,8,1,4,1,1536]{5,3,2,1,0,4:T(4,128)} %get-tuple-element.78) | copy-start | bytes 2359300
  75.8 3.4 %copy-start.2 = (f32[4,8,8,1,1536]{4,2,1,0,3:T(8,128)S(1)}, f32[4,8,8,1,1536]{4,2,1,0,3:T(8,128)}, u32[]{:S(2)}) copy-start(f32[4,8,8,1,1536]{4,2,1,0,3:T(8,128)} %stack.50) | copy-start | bytes 4718596
  75.8 3.4 %copy-start.6 = (f32[4,8,8,1,47]{4,2,3,1,0:T(8,128)S(1)}, f32[4,8,8,1,47]{4,2,3,1,0:T(8,128)}, u32[]{:S(2)}) copy-start(f32[4,8,8,1,47]{4,2,3,1,0:T(8,128)} %get-tuple-element.65) | copy-start | bytes 144388
  75.8 3.4 %copy-start.7 = (f32[4,8,8,1,47]{4,2,3,1,0:T(8,128)S(1)}, f32[4,8,8,1,47]{4,2,3,1,0:T(8,128)}, u32[]{:S(2)}) copy-start(f32[4,8,8,1,47]{4,2,3,1,0:T(8,128)} %get-tuple-element.66) | copy-start | bytes 144388
  75.8 3.4 %copy-start.8 = (f32[4,8,8,1,1]{4,2,3,1,0:T(8,128)S(1)}, f32[4,8,8,1,1]{4,2,3,1,0:T(8,128)}, u32[]{:S(2)}) copy-start(f32[4,8,8,1,1]{4,2,3,1,0:T(8,128)} %get-tuple-element.59) | copy-start | bytes 3076
  75.8 3.4 %copy-start.12 = (f32[1536]{0:T(1024)S(1)}, f32[1536]{0:T(1024)}, u32[]{:S(2)}) copy-start(f32[1536]{0:T(1024)} %get-tuple-element.71) | copy-start | bytes 18436
  75.8 3.4 %copy-start.18 = (pred[1536]{0:T(1024)(128)(4,1)S(1)}, pred[1536]{0:T(1024)(128)(4,1)}, u32[]{:S(2)}) copy-start(pred[1536]{0:T(1024)(128)(4,1)} %get-tuple-element.84) | copy-start | bytes 4612
  75.8 3.4 %copy-start.19 = (pred[1536]{0:T(1024)(128)(4,1)S(1)}, pred[1536]{0:T(1024)(128)(4,1)}, u32[]{:S(2)}) copy-start(pred[1536]{0:T(1024)(128)(4,1)} %get-tuple-element.85) | copy-start | bytes 4612
where the time goes:
time: 128 us
  other arithmetic  33.6 us (26%)
  blocking collectives  33.6 us (26%)
  local copies, waits for them, and re-layouts  32.4 us (25%)
  matrix products  14.5 us (11%)
  starting transfers between devices  11.8 us (9%)
  between operations  1.66 us (1%)
    all_to_all x2, blocking collectives, copy_for_each(): return lax.all_to_all(copies, axis, split_axis=0, concat_axis=0, tiled=True)  33.6 us
    another operation x7, local copies, waits for them, and re-layouts, coupling(): jnp.stack([base_re * mix_re - base_im * mix_im, base_re * mix_im + base_i...  11.9 us
    dot_general x7, matrix products, coupling(): jnp.einsum('vw,...cwxn->...cvxn', mixing[j], halves, precision=lax.Precis...  11.5 us
    convert_element_type x1, other arithmetic, local(): response = result.astype(jnp.bfloat16)  11 us
    another operation x7, local copies, waits for them, and re-layouts  6.95 us
    another operation x7, other arithmetic, coupling(): jnp.stack([base_re * mix_re - base_im * mix_im, base_re * mix_im + base_i...  6.26 us
    sub x4, other arithmetic, coupling(): base_re * mix_re - base_im * mix_im  5.56 us
    ppermute x1, starting transfers between devices, with_halo(): lax.ppermute(head, axis, [((i + 1) % count, i) for i in range(ends)])  5.15 us
  transfers between devices with their start and end apart: 4, of which 0 were waited for; matrix products, arithmetic and copies ran while one was open for 51% of the time, Pallas kernels for 0%

commit v1 on v0

v1 whole, which is shorter than its diff:
```python
import functools

import jax
import jax.numpy as jnp
from jax import lax
from jax.experimental import pallas as pl
from jax.experimental.pallas import tpu as pltpu
from jax.sharding import PartitionSpec as P

MESH = pl.DeviceIdType.MESH
S, K, C, N = 4, 8, 8, 1536
ROWS = K * C
NZ = 48
OMEGA = 0.05
VISCOSITY = 0.25
CHUNKS = 4
CROWS = ROWS // CHUNKS
RIM = 3 * C
LANES = 256

OWN = [(j, k, k - j + 3) for k in range(K) for j in range(7) if 0 <= k - j + 3 < K]
LEFT = [(j, k, k - j + 6) for k in range(3) for j in range(7) if k - j + 3 < 0]
RIGHT = [(j, k, k - j + 3 - K) for k in range(K - 3, K) for j in range(7) if k - j + 3 >= K]

PAIRS = [(s, t) for s in range(S) for t in range(s, S)]


def split(coeff):
    high = coeff.astype(jnp.bfloat16)
    low = (coeff - high.astype(jnp.float32)).astype(jnp.bfloat16)
    return high, low


def swapped(value):
    return jnp.concatenate([value[4:], value[:4]], axis=0)


def pair_iota(width):
    row = lax.broadcasted_iota(jnp.int32, (C, width), 0)
    col = lax.broadcasted_iota(jnp.int32, (C, width), 1)
    return row, col


def mixing_tile(mix_ref, j, width):
    row, col = pair_iota(width)
    same = (row // 4) == ((col // 4) % 2)
    tile = jnp.zeros((C, width), jnp.float32)
    for v in range(4):
        for w in range(4):
            hit = same & (row % 4 == v) & (col % 4 == w)
            tile = jnp.where(hit, mix_ref[v, w, j], tile)
    return tile


def halo_kernel(
    f_ref, blocks_ref, base_ref, mean_ref, mix_hbm, lo_hbm, flag_hbm, resp_ref, part_ref,
    mix_ref, lo_ref, flag_ref,
    x_ref, from_left, from_right, rim_in, base_in, mean_in, re_ref, im_ref,
    acc_ref, out_ref, own_coeff, rim_coeff, mixed_ref, rim_mixed, gram_ref,
    in_sem, out_sem, send_sem, recv_sem, rim_send, rim_recv,
):
    sp, fr = lax.axis_index("space"), lax.axis_index("freq")
    has_l, has_r = sp > 0, sp < lax.axis_size("space") - 1
    has_d, has_u = fr > 0, fr < lax.axis_size("freq") - 1
    to_l, to_r = {"space": sp - 1}, {"space": sp + 1}
    to_d, to_u = {"freq": fr - 1}, {"freq": fr + 1}
    greeted = ((has_l, to_l), (has_r, to_r), (has_d, to_d), (has_u, to_u))

    barrier = pltpu.get_barrier_semaphore()
    for there, device in greeted:

        @pl.when(there)
        def _():
            pl.semaphore_signal(barrier, inc=1, device_id=device, device_id_type=MESH)

    load_x = pltpu.make_async_copy(f_ref, x_ref, in_sem.at[0])
    load_base = pltpu.make_async_copy(base_ref, base_in, in_sem.at[1])
    load_mean = pltpu.make_async_copy(mean_ref, mean_in, in_sem.at[2])
    loads = [load_x, load_base, load_mean]
    for i, (source, target) in enumerate(
        ((mix_hbm, mix_ref), (lo_hbm, lo_ref), (flag_hbm, flag_ref))
    ):
        loads.append(pltpu.make_async_copy(source, target, in_sem.at[3 + i]))
    for load in loads:
        load.start()
    peers = sum(there.astype(jnp.int32) for there, _ in greeted)
    pl.semaphore_wait(barrier, peers)

    def plane_copy(way, part):
        rows = pl.ds(part * CROWS, CROWS)
        landing = from_left if way == 0 else from_right
        return pltpu.make_async_remote_copy(
            src_ref=f_ref.at[:, rows],
            dst_ref=landing.at[:, rows],
            send_sem=send_sem.at[way, part],
            recv_sem=recv_sem.at[way, part],
            device_id=to_r if way == 0 else to_l,
            device_id_type=MESH,
        )

    def rim_copy(way):
        return pltpu.make_async_remote_copy(
            src_ref=blocks_ref.at[:, K - 3 : K] if way == 0 else blocks_ref.at[:, 0:3],
            dst_ref=rim_in.at[way],
            send_sem=rim_send.at[way],
            recv_sem=rim_recv.at[way],
            device_id=to_u if way == 0 else to_d,
            device_id_type=MESH,
        )

    for way, there in ((0, has_u), (1, has_d)):

        @pl.when(there)
        def _():
            rim_copy(way).start()

    for part in range(CHUNKS):
        for way, there in ((0, has_r), (1, has_l)):

            @pl.when(there)
            def _():
                plane_copy(way, part).start()

    for way, there in ((0, has_d), (1, has_u)):

        @pl.when(jnp.logical_not(there))
        def _():
            rim_in[way] = jnp.zeros((S, 3, C, N), jnp.bfloat16)

    for landing, there in ((from_left, has_l), (from_right, has_r)):

        @pl.when(jnp.logical_not(there))
        def _():
            landing[...] = jnp.zeros((S, ROWS, N), jnp.bfloat16)

    for load in loads:
        load.wait()
    width = S * RIM
    row, col = pair_iota(width)
    for j in range(7):
        tile = mixing_tile(mix_ref, j, width)
        for slot, (jj, k, source) in enumerate(OWN):
            if jj == j:
                flag = flag_ref[k, j].astype(jnp.float32)
                block = jnp.where(col // C == source, tile, 0.0) * flag
                own_coeff[slot * C : slot * C + C, :] = block[:, :ROWS]
        for way, listed in ((0, LEFT), (1, RIGHT)):
            for slot, (jj, k, source) in enumerate(listed):
                if jj == j:
                    flag = flag_ref[k, j].astype(jnp.float32)
                    for s in range(S):
                        at = (s * len(listed) + slot) * C
                        block = jnp.where(col // C == 3 * s + source, tile, 0.0) * flag
                        rim_coeff[way, at : at + C, :] = block

    for j in range(7):
        re_ref[j] = jnp.broadcast_to(base_in[j, 0], (C, N))
        im_ref[j] = jnp.broadcast_to(base_in[j, 1], (C, N))

    own_high, own_low = split(own_coeff[...])
    own_both = jnp.concatenate([own_high, own_low], axis=1)
    sign = jnp.where(lax.broadcasted_iota(jnp.int32, (C, N), 0) < 4, 1.0, -1.0).astype(jnp.float32)
    first = lo_ref[0] + fr * K

    place = lax.broadcasted_iota(jnp.int32, (C, N), 1)
    span = place % NZ
    span_last, span_first = span == NZ - 1, span == 0
    wake_last, wake_first = place >= N - NZ, place < NZ

    def local_part(s, carry):
        values = x_ref[s]
        mixed_ref[...] = jnp.dot(
            own_both,
            jnp.concatenate([values, values], axis=0),
            preferred_element_type=jnp.float32,
        )
        for k in range(K):
            if k % 2 == 0:
                both = x_ref[s, k * C : k * C + 2 * C].astype(jnp.float32)
            x = both[(k % 2) * C : (k % 2) * C + C]
            up, down = pltpu.roll(x, N - 1, 1), pltpu.roll(x, 1, 1)
            span_up = jnp.where(span_last, pltpu.roll(x, NZ - 1, 1), up)
            span_down = jnp.where(span_first, pltpu.roll(x, N - NZ + 1, 1), down)
            wake_up = jnp.where(wake_last, 0.0, pltpu.roll(x, N - NZ, 1))
            wake_down = jnp.where(wake_first, 0.0, pltpu.roll(x, NZ, 1))
            around = VISCOSITY * (wake_up + wake_down + span_up + span_down - 6.0 * x)
            spin = OMEGA * (first + k).astype(jnp.float32)
            turned = spin * x
            straight = around
            for slot, (j, kk, _source) in enumerate(OWN):
                if kk == k:
                    mixed = mixed_ref[slot * C : slot * C + C, :]
                    straight = straight + re_ref[j] * mixed
                    turned = turned - im_ref[j] * mixed
            acc_ref[s, k * C : k * C + C] = swapped(sign * turned) - straight
        return carry

    lax.fori_loop(0, S, local_part, 0)

    for way, there, listed in ((0, has_d, LEFT), (1, has_u, RIGHT)):

        @pl.when(there)
        def _():
            rim_copy(way).wait_recv()

        high, low = split(rim_coeff[way])
        rim = rim_in[way].astype(jnp.float32).reshape(S * RIM, N).astype(jnp.bfloat16)
        rim_mixed[...] = jnp.dot(high, rim, preferred_element_type=jnp.float32) + jnp.dot(
            low, rim, preferred_element_type=jnp.float32
        )

        def rim_part(s, carry):
            for k in sorted({k for _, k, _ in listed}):
                straight = turned = None
                for slot, (j, kk, _source) in enumerate(listed):
                    if kk == k:
                        at = pl.multiple_of((s * len(listed) + slot) * C, C)
                        mixed = rim_mixed[pl.ds(at, C), :]
                        a, b = re_ref[j] * mixed, im_ref[j] * mixed
                        straight = a if straight is None else straight + a
                        turned = b if turned is None else turned + b
                acc_ref[s, k * C : k * C + C] -= swapped(sign * turned) + straight
            return carry

        lax.fori_loop(0, S, rim_part, 0)

    gram_ref[...] = jnp.zeros_like(gram_ref)
    half = 0.5 * mean_in[...].reshape(1, N)
    for part in range(CHUNKS):
        rows = slice(part * CROWS, (part + 1) * CROWS)
        for way, there in ((0, has_l), (1, has_r)):

            @pl.when(there)
            def _():
                plane_copy(way, part).wait_recv()

        sums = [gram_ref[p] for p in range(len(PAIRS))]
        for at in range(0, N, LANES):
            lanes = slice(at, at + LANES)
            gain_l = VISCOSITY + half[:, lanes]
            gain_r = VISCOSITY - half[:, lanes]
            rounded = []
            for s in range(S):
                left = from_left[s, rows, lanes].astype(jnp.float32)
                right = from_right[s, rows, lanes].astype(jnp.float32)
                value = acc_ref[s, rows, lanes] - (gain_l * left + gain_r * right)
                value = value.astype(jnp.bfloat16)
                out_ref[s, rows, lanes] = value
                rounded.append(value.astype(jnp.float32))
            for p, (s, t) in enumerate(PAIRS):
                product = rounded[s] * rounded[t]
                sums[p] = sums[p] + (product[:C] + product[C:])
        for p in range(len(PAIRS)):
            gram_ref[p] = sums[p]
        pltpu.make_async_copy(
            out_ref.at[:, rows], resp_ref.at[:, rows], out_sem.at[part]
        ).start()

    row, col = pair_iota(128)
    tile = jnp.zeros((C, 128), jnp.float32)
    for p, (s, t) in enumerate(PAIRS):
        total = jnp.sum(gram_ref[p])
        hit = ((row == s) & (col == t)) | ((row == t) & (col == s))
        tile = jnp.where(hit, total, tile)
    part_ref[...] = tile

    for part in range(CHUNKS):
        rows = slice(part * CROWS, (part + 1) * CROWS)
        pltpu.make_async_copy(
            out_ref.at[:, rows], resp_ref.at[:, rows], out_sem.at[part]
        ).wait()
        for way, there in ((0, has_r), (1, has_l)):

            @pl.when(there)
            def _():
                plane_copy(way, part).wait_send()

    for way, there in ((0, has_u), (1, has_d)):

        @pl.when(there)
        def _():
            rim_copy(way).wait_send()


def apply_operator(forcing, base_harm, mean_flow, mixing, harm_lo, couple_flags):
    any_ = pl.BlockSpec(memory_space=pl.ANY)
    bf16, f32 = jnp.bfloat16, jnp.float32
    return pl.pallas_call(
        halo_kernel,
        out_shape=(
            jax.ShapeDtypeStruct((S, ROWS, N), bf16),
            jax.ShapeDtypeStruct((C, 128), f32),
        ),
        in_specs=[any_] * 7,
        out_specs=(any_, pl.BlockSpec(memory_space=pltpu.VMEM)),
        scratch_shapes=[
            pltpu.SMEM((4, 4, 7), f32),
            pltpu.SMEM((1,), jnp.int32),
            pltpu.SMEM((K, 7), jnp.int32),
            pltpu.VMEM((S, ROWS, N), bf16),
            pltpu.VMEM((S, ROWS, N), bf16),
            pltpu.VMEM((S, ROWS, N), bf16),
            pltpu.VMEM((2, S, 3, C, N), bf16),
            pltpu.VMEM((7, 2, 1, N), f32),
            pltpu.VMEM((N,), f32),
            pltpu.VMEM((7, C, N), f32),
            pltpu.VMEM((7, C, N), f32),
            pltpu.VMEM((S, ROWS, N), f32),
            pltpu.VMEM((S, ROWS, N), bf16),
            pltpu.VMEM((len(OWN) * C, ROWS), f32),
            pltpu.VMEM((2, S * len(LEFT) * C, S * RIM), f32),
            pltpu.VMEM((len(OWN) * C, N), f32),
            pltpu.VMEM((S * len(LEFT) * C, N), f32),
            pltpu.VMEM((len(PAIRS), C, LANES), f32),
            pltpu.SemaphoreType.DMA((6,)),
            pltpu.SemaphoreType.DMA((CHUNKS,)),
            pltpu.SemaphoreType.DMA((2, CHUNKS)),
            pltpu.SemaphoreType.DMA((2, CHUNKS)),
            pltpu.SemaphoreType.DMA((2,)),
            pltpu.SemaphoreType.DMA((2,)),
        ],
        compiler_params=pltpu.CompilerParams(
            collective_id=0, has_side_effects=True, vmem_limit_bytes=56 << 20
        ),
        name="operator",
    )(forcing.reshape(S, ROWS, N), forcing.reshape(S, K, C, N), base_harm, mean_flow, mixing, harm_lo, couple_flags)


def solution(mesh):
    n_space, n_freq = mesh.shape["space"], mesh.shape["freq"]
    cells_all = S * K * n_freq * C * n_space * N // S
    y, xh, core, xl = 4, 2, 2, 2
    z = n_space // (xh * y)
    sizes = {"z": z, "xh": xh, "y": y, "xl": xl, "core": core}
    stages = [("z", "core"), ("xh", "xl", "y")]
    counts = []
    for axes in stages:
        count = 1
        for axis in axes:
            count *= sizes[axis]
        counts.append(count - 1)

    def gram_kernel(part_ref, gram_ref, mine, *rest):
        landing, send_sem, recv_sem = rest[:2], rest[2:4], rest[4:6]
        sp, fr = lax.axis_index("space"), lax.axis_index("freq")
        here = {
            "z": sp // (xh * y), "xh": sp // y % xh, "y": sp % y,
            "xl": fr // core, "core": fr % core,
        }

        def partner(axes, step):
            there = dict(here)
            for axis in axes:
                there[axis] = lax.rem(here[axis] + step % sizes[axis], sizes[axis])
                step //= sizes[axis]
            space = (there["z"] * xh + there["xh"]) * y + there["y"]
            return {"space": space, "freq": there["xl"] * core + there["core"]}

        barrier = pltpu.get_barrier_semaphore()
        for axes, count in zip(stages, counts):
            for step in range(1, count + 1):
                pl.semaphore_signal(
                    barrier, inc=1, device_id=partner(axes, step), device_id_type=MESH
                )
        pl.semaphore_wait(barrier, sum(counts))
        total = part_ref[...]
        for i, (axes, count) in enumerate(zip(stages, counts)):
            mine[i] = total
            copies = []
            for step in range(1, count + 1):
                copy = pltpu.make_async_remote_copy(
                    src_ref=mine.at[i],
                    dst_ref=landing[i].at[step - 1],
                    send_sem=send_sem[i].at[step - 1],
                    recv_sem=recv_sem[i].at[step - 1],
                    device_id=partner(axes, step),
                    device_id_type=MESH,
                )
                copy.start()
                copies.append(copy)
            for copy in copies:
                copy.wait_recv()
            total = total + jnp.sum(landing[i][...], axis=0)
            for copy in copies:
                copy.wait_send()
        gram_ref[...] = total[:S, :S] / cells_all

    def gram_sum(part):
        f32 = jnp.float32
        return pl.pallas_call(
            gram_kernel,
            out_shape=jax.ShapeDtypeStruct((S, S), f32),
            in_specs=[pl.BlockSpec(memory_space=pltpu.VMEM)],
            out_specs=pl.BlockSpec(memory_space=pltpu.VMEM),
            scratch_shapes=[pltpu.VMEM((2, C, 128), f32)]
            + [pltpu.VMEM((count, C, 128), f32) for count in counts]
            + [pltpu.SemaphoreType.DMA((count,)) for count in counts] * 2,
            compiler_params=pltpu.CompilerParams(collective_id=1, has_side_effects=True),
            name="gram_sum",
        )(part)

    def local(forcing, base_harm, mixing, mean_flow, harm_lo, couple_flags):
        shape = forcing.shape
        response, part = apply_operator(
            forcing,
            base_harm,
            mean_flow,
            mixing.transpose(1, 2, 0),
            harm_lo,
            couple_flags,
        )
        return response.reshape(shape), gram_sum(part)

    return jax.shard_map(
        local,
        mesh=mesh,
        in_specs=(
            P(None, "freq", None, "space", None),
            P(None, None, "space", None),
            P(),
            P(),
            P(),
            P("freq", None),
        ),
        out_specs=(P(None, "freq", None, "space", None), P()),
        check_vma=False,
    )
```

time: 128 us -> 54.4 us (0.42)
  Pallas kernels: 0 us -> 50.2 us
  other arithmetic: 33.6 us -> 0 us
  blocking collectives: 33.6 us -> 0 us
  local copies, waits for them, and re-layouts: 32.4 us -> 2.65 us
  matrix products: 14.5 us -> 0 us
  starting transfers between devices: 11.8 us -> 0 us
    pallas_call x0 -> x2, Pallas kernels: none -> 50.2 us  [the longest x1 28.7 us: apply_operator(): pl.pallas_call(halo_kernel, out_shape=(jax.ShapeDtypeStruct((S, ROWS, N),...]
    all_to_all x2 -> x0, blocking collectives: 33.6 us -> none  [copy_for_each(): return lax.all_to_all(copies, axis, split_axis=0, concat_axis=0, tiled=True)]
    another operation x14 -> x0, local copies, waits for them, and re-layouts: 18.9 us -> none  [the longest x7 11.9 us: coupling(): jnp.stack([base_re * mix_re - base_im * mix_im, base_re * mix_im + base_i...]
    dot_general x8 -> x0, matrix products: 14.5 us -> none  [the longest x7 11.5 us: coupling(): jnp.einsum('vw,...cwxn->...cvxn', mixing[j], halves, precision=lax.Precis...]
    slice x11 -> x0, local copies, waits for them, and re-layouts: 13.3 us -> none  [the longest x2 2.89 us: crossflow(): jnp.roll(values, 1 - NZ, -1)]
    convert_element_type x3 -> x0, other arithmetic: 13.2 us -> none  [the longest x1 11 us: local(): response = result.astype(jnp.bfloat16)]
    ppermute x4 -> x0, starting transfers between devices: 11.8 us -> none  [the longest x1 5.15 us: with_halo(): lax.ppermute(head, axis, [((i + 1) % count, i) for i in range(ends)])]
    another operation x7 -> x0, other arithmetic: 6.26 us -> none  [coupling(): jnp.stack([base_re * mix_re - base_im * mix_im, base_re * mix_im + base_i...]
  transfers between devices with their start and end apart: 4 -> 0, of which waited for: 0 -> 0; matrix products, arithmetic and copies ran while one was open for 51% -> 0% of each run, Pallas kernels for 0% -> 0%
where the time goes in v1:
time: 54.4 us; the launch traced here: 54.2 us
  Pallas kernels  50.2 us (92%)
  local copies, waits for them, and re-layouts  2.65 us (5%)
  between operations  1.3 us (2%)
    pallas_call x1, Pallas kernels, apply_operator(): pl.pallas_call(halo_kernel, out_shape=(jax.ShapeDtypeStruct((S, ROWS, N),...  28.7 us
    pallas_call x1, Pallas kernels, gram_sum(): pl.pallas_call(gram_kernel, out_shape=jax.ShapeDtypeStruct((S, S), f32),...  21.5 us
    unnamed x4, local copies, waits for them, and re-layouts  2.65 us

profile of v1, /device:TPU:1, one launch (start us, length us, event | category | flops | bytes accessed | tf_op | source)
XLA Modules:
  0.0 54.2 jit_solution(15532128001867484448)
XLA Ops:
  1.3 28.7 %operator.1 = (bf16[4,64,1536]{2,1,0:T(8,128)(2,1)}, f32[8,128]{1,0:T(8,128)}) custom-call(bf16[4,64,1536]{2,1,0:T(8,128)(2,1)} %bitcast.6, bf16[4,8,8,1536]{3,2,1,0:T(8,128)(2,1)} %bitcast.7, f32[7,2,1,1536]{3,2,1,0:T(1,128)} %base_ref.1, f32[1536]{0:T(1024)} %mean_ref.1, f32[4,4,7]{2,1,0:T(4,128)} %bitcast.9, s32[1]{0:T(128)S(6)} %copy.11.lo_hbm, ...), custom_call_target="tpu_custom_call" | custom-call | tf_op jit(solution)/shard_map/operator/pallas_call | solution.py:288
  30.0 21.5 %gram_sum.1 = f32[4,4]{1,0:T(4,128)} custom-call(f32[8,128]{1,0:T(8,128)} %get-tuple-element.5.part_ref), custom_call_target="tpu_custom_call" | custom-call | tf_op jit(solution)/shard_map/gram_sum/pallas_call | solution.py:390
  51.5 0.0 copy-start
  51.5 2.1 %copy.12 = bf16[4,8,8,1,1536]{4,2,3,1,0:T(8,128)(2,1)} copy(bf16[4,8,8,1,1536]{4,2,3,1,0:T(8,128)(2,1)} %bitcast.8) | data formatting | bytes 1572864
  53.6 0.0 copy-done
  53.6 0.6 %copy.13 = f32[4,4]{1,0:T(4,128)} copy(f32[4,4]{1,0:T(4,128)S(1)} %copy-done) | data formatting | bytes 128
Async XLA Ops:
  51.5 2.1 %copy-start = (f32[4,4]{1,0:T(4,128)S(1)}, f32[4,4]{1,0:T(4,128)}, u32[]{:S(2)}) copy-start(f32[4,4]{1,0:T(4,128)} %gram_sum.1) | copy-start | bytes 196

commit v2 on v1

--- a/solution.py
+++ b/solution.py
@@ -16,6 +16,8 @@
 CHUNKS = 4
 CROWS = ROWS // CHUNKS
 RIM = 3 * C
+Y = 4
+DIRECT = 2
 LANES = 256
 
 OWN = [(j, k, k - j + 3) for k in range(K) for j in range(7) if 0 <= k - j + 3 < K]
@@ -55,16 +57,22 @@
 def halo_kernel(
     f_ref, blocks_ref, base_ref, mean_ref, mix_hbm, lo_hbm, flag_hbm, resp_ref, part_ref,
     mix_ref, lo_ref, flag_ref,
-    x_ref, from_left, from_right, rim_in, base_in, mean_in, re_ref, im_ref,
-    acc_ref, out_ref, own_coeff, rim_coeff, mixed_ref, rim_mixed, gram_ref,
-    in_sem, out_sem, send_sem, recv_sem, rim_send, rim_recv,
+    x_ref, from_left, from_right, rim_in, relay, base_in, mean_in, re_ref, im_ref,
+    acc_ref, own_coeff, rim_coeff, mixed_ref, rim_mixed, gram_ref,
+    in_sem, send_sem, recv_sem, rim_send, rim_recv, relay_sem,
 ):
     sp, fr = lax.axis_index("space"), lax.axis_index("freq")
     has_l, has_r = sp > 0, sp < lax.axis_size("space") - 1
     has_d, has_u = fr > 0, fr < lax.axis_size("freq") - 1
     to_l, to_r = {"space": sp - 1}, {"space": sp + 1}
     to_d, to_u = {"freq": fr - 1}, {"freq": fr + 1}
-    greeted = ((has_l, to_l), (has_r, to_r), (has_d, to_d), (has_u, to_u))
+    edge = jnp.logical_or(sp % Y == 0, sp % Y == Y - 1)
+    middle = jnp.logical_not(edge)
+    up_hop, down_hop = fr == 1, fr == 2
+    hop = jnp.logical_or(up_hop, down_hop)
+    next_row = {"space": sp + 1 - 2 * (sp % 2)}
+    across = {"space": sp + 1 - 2 * (sp % 2), "freq": 3 - fr}
+    greeted = ((has_l, to_l), (has_r, to_r), (has_d, to_d), (has_u, to_u), (hop, across))
 
     barrier = pltpu.get_barrier_semaphore()
     for there, device in greeted:
@@ -98,28 +106,64 @@
             device_id_type=MESH,
         )
 
-    def rim_copy(way):
+    def rim_of(way, low, high):
+        first = K - 3 if way == 0 else 0
+        return blocks_ref.at[low:high, first : first + 3]
+
+    def rim_copy(way, low=0, high=S):
         return pltpu.make_async_remote_copy(
-            src_ref=blocks_ref.at[:, K - 3 : K] if way == 0 else blocks_ref.at[:, 0:3],
-            dst_ref=rim_in.at[way],
+            src_ref=rim_of(way, low, high),
+            dst_ref=rim_in.at[way, low:high],
             send_sem=rim_send.at[way],
             recv_sem=rim_recv.at[way],
             device_id=to_u if way == 0 else to_d,
             device_id_type=MESH,
         )
 
-    for way, there in ((0, has_u), (1, has_d)):
-
-        @pl.when(there)
+    def to_relay(way):
+        return pltpu.make_async_remote_copy(
+            src_ref=rim_of(way, DIRECT, S),
+            dst_ref=relay,
+            send_sem=relay_sem.at[0],
+            recv_sem=relay_sem.at[1],
+            device_id=next_row,
+            device_id_type=MESH,
+        )
+
+    def from_relay(way):
+        return pltpu.make_async_remote_copy(
+            src_ref=relay,
+            dst_ref=rim_in.at[way, DIRECT:],
+            send_sem=relay_sem.at[2],
+            recv_sem=relay_sem.at[3],
+            device_id=across,
+            device_id_type=MESH,
+        )
+
+    def when(*conditions):
+        return pl.when(functools.reduce(jnp.logical_and, conditions))
+
+    for way, there, far in ((0, has_u, up_hop), (1, has_d, down_hop)):
+        split_up = jnp.logical_and(edge, far)
+
+        @when(there, jnp.logical_not(split_up))
         def _():
             rim_copy(way).start()
 
-    for part in range(CHUNKS):
-        for way, there in ((0, has_r), (1, has_l)):
-
-            @pl.when(there)
-            def _():
-                plane_copy(way, part).start()
+        @when(split_up)
+        def _():
+            to_relay(way).start()
+            rim_copy(way, 0, DIRECT).start()
+
+    def start_planes(parts):
+        for part in parts:
+            for way, there in ((0, has_r), (1, has_l)):
+
+                @when(there)
+                def _():
+                    plane_copy(way, part).start()
+
+    start_planes(range(CHUNKS // 2))
 
     for way, there in ((0, has_d), (1, has_u)):
 
@@ -156,6 +200,18 @@
     for j in range(7):
         re_ref[j] = jnp.broadcast_to(base_in[j, 0], (C, N))
         im_ref[j] = jnp.broadcast_to(base_in[j, 1], (C, N))
+
+    @when(middle, hop)
+    def _():
+        to_relay(0).wait_recv()
+
+    for way, far in ((0, up_hop), (1, down_hop)):
+
+        @when(middle, far)
+        def _():
+            from_relay(way).start()
+
+    start_planes(range(CHUNKS // 2, CHUNKS))
 
     own_high, own_low = split(own_coeff[...])
     own_both = jnp.concatenate([own_high, own_low], axis=1)
@@ -197,11 +253,17 @@
 
     lax.fori_loop(0, S, local_part, 0)
 
-    for way, there, listed in ((0, has_d, LEFT), (1, has_u, RIGHT)):
-
-        @pl.when(there)
+    for way, there, far, listed in ((0, has_d, down_hop, LEFT), (1, has_u, up_hop, RIGHT)):
+        split_up = jnp.logical_and(edge, far)
+
+        @when(there, jnp.logical_not(split_up))
         def _():
             rim_copy(way).wait_recv()
+
+        @when(split_up)
+        def _():
+            rim_copy(way, 0, DIRECT).wait_recv()
+            from_relay(way).wait_recv()
 
         high, low = split(rim_coeff[way])
         rim = rim_in[way].astype(jnp.float32).reshape(S * RIM, N).astype(jnp.bfloat16)
@@ -245,16 +307,13 @@
                 right = from_right[s, rows, lanes].astype(jnp.float32)
                 value = acc_ref[s, rows, lanes] - (gain_l * left + gain_r * right)
                 value = value.astype(jnp.bfloat16)
-                out_ref[s, rows, lanes] = value
+                resp_ref[s, rows, lanes] = value
                 rounded.append(value.astype(jnp.float32))
             for p, (s, t) in enumerate(PAIRS):
                 product = rounded[s] * rounded[t]
                 sums[p] = sums[p] + (product[:C] + product[C:])
         for p in range(len(PAIRS)):
             gram_ref[p] = sums[p]
-        pltpu.make_async_copy(
-            out_ref.at[:, rows], resp_ref.at[:, rows], out_sem.at[part]
-        ).start()
 
     row, col = pair_iota(128)
     tile = jnp.zeros((C, 128), jnp.float32)
@@ -265,34 +324,40 @@
     part_ref[...] = tile
 
     for part in range(CHUNKS):
-        rows = slice(part * CROWS, (part + 1) * CROWS)
-        pltpu.make_async_copy(
-            out_ref.at[:, rows], resp_ref.at[:, rows], out_sem.at[part]
-        ).wait()
         for way, there in ((0, has_r), (1, has_l)):
 
             @pl.when(there)
             def _():
                 plane_copy(way, part).wait_send()
 
-    for way, there in ((0, has_u), (1, has_d)):
-
-        @pl.when(there)
+    for way, there, far in ((0, has_u, up_hop), (1, has_d, down_hop)):
+        split_up = jnp.logical_and(edge, far)
+
+        @when(there, jnp.logical_not(split_up))
         def _():
             rim_copy(way).wait_send()
 
+        @when(split_up)
+        def _():
+            rim_copy(way, 0, DIRECT).wait_send()
+            to_relay(way).wait_send()
+
+        @when(middle, far)
+        def _():
+            from_relay(way).wait_send()
+
 
 def apply_operator(forcing, base_harm, mean_flow, mixing, harm_lo, couple_flags):
-    any_ = pl.BlockSpec(memory_space=pl.ANY)
+    hbm, vmem = pl.BlockSpec(memory_space=pltpu.HBM), pl.BlockSpec(memory_space=pltpu.VMEM)
     bf16, f32 = jnp.bfloat16, jnp.float32
     return pl.pallas_call(
         halo_kernel,
         out_shape=(
-            jax.ShapeDtypeStruct((S, ROWS, N), bf16),
-            jax.ShapeDtypeStruct((C, 128), f32),
+            pltpu.VMEM((S, ROWS, N), bf16),
+            pltpu.VMEM((C, 128), f32),
         ),
-        in_specs=[any_] * 7,
-        out_specs=(any_, pl.BlockSpec(memory_space=pltpu.VMEM)),
+        in_specs=[hbm] * 7,
+        out_specs=(vmem, vmem),
         scratch_shapes=[
             pltpu.SMEM((4, 4, 7), f32),
             pltpu.SMEM((1,), jnp.int32),
@@ -301,26 +366,26 @@
             pltpu.VMEM((S, ROWS, N), bf16),
             pltpu.VMEM((S, ROWS, N), bf16),
             pltpu.VMEM((2, S, 3, C, N), bf16),
+            pltpu.VMEM((S - DIRECT, 3, C, N), bf16),
             pltpu.VMEM((7, 2, 1, N), f32),
             pltpu.VMEM((N,), f32),
             pltpu.VMEM((7, C, N), f32),
             pltpu.VMEM((7, C, N), f32),
             pltpu.VMEM((S, ROWS, N), f32),
-            pltpu.VMEM((S, ROWS, N), bf16),
             pltpu.VMEM((len(OWN) * C, ROWS), f32),
             pltpu.VMEM((2, S * len(LEFT) * C, S * RIM), f32),
             pltpu.VMEM((len(OWN) * C, N), f32),
             pltpu.VMEM((S * len(LEFT) * C, N), f32),
             pltpu.VMEM((len(PAIRS), C, LANES), f32),
             pltpu.SemaphoreType.DMA((6,)),
-            pltpu.SemaphoreType.DMA((CHUNKS,)),
             pltpu.SemaphoreType.DMA((2, CHUNKS)),
             pltpu.SemaphoreType.DMA((2, CHUNKS)),
             pltpu.SemaphoreType.DMA((2,)),
             pltpu.SemaphoreType.DMA((2,)),
+            pltpu.SemaphoreType.DMA((4,)),
         ],
         compiler_params=pltpu.CompilerParams(
-            collective_id=0, has_side_effects=True, vmem_limit_bytes=56 << 20
+            collective_id=0, has_side_effects=True, vmem_limit_bytes=62 << 20
         ),
         name="operator",
     )(forcing.reshape(S, ROWS, N), forcing.reshape(S, K, C, N), base_harm, mean_flow, mixing, harm_lo, couple_flags)
@@ -333,12 +398,22 @@
     z = n_space // (xh * y)
     sizes = {"z": z, "xh": xh, "y": y, "xl": xl, "core": core}
     stages = [("z", "core"), ("xh", "xl", "y")]
-    counts = []
+    counts, orders = [], []
+
+    def hops(axes, step):
+        total = 0
+        for axis in reversed(axes):
+            by = step % sizes[axis]
+            total += (2 if axis == "xh" else 1) * min(by, sizes[axis] - by)
+            step //= sizes[axis]
+        return total
+
     for axes in stages:
         count = 1
         for axis in axes:
             count *= sizes[axis]
         counts.append(count - 1)
+        orders.append(sorted(range(1, count), key=lambda step: -hops(axes, step)))
 
     def gram_kernel(part_ref, gram_ref, mine, *rest):
         landing, send_sem, recv_sem = rest[:2], rest[2:4], rest[4:6]
@@ -350,24 +425,24 @@
 
         def partner(axes, step):
             there = dict(here)
-            for axis in axes:
+            for axis in reversed(axes):
                 there[axis] = lax.rem(here[axis] + step % sizes[axis], sizes[axis])
                 step //= sizes[axis]
             space = (there["z"] * xh + there["xh"]) * y + there["y"]
             return {"space": space, "freq": there["xl"] * core + there["core"]}
 
         barrier = pltpu.get_barrier_semaphore()
-        for axes, count in zip(stages, counts):
-            for step in range(1, count + 1):
+        for axes, order in zip(stages, orders):
+            for step in order:
                 pl.semaphore_signal(
                     barrier, inc=1, device_id=partner(axes, step), device_id_type=MESH
                 )
         pl.semaphore_wait(barrier, sum(counts))
         total = part_ref[...]
-        for i, (axes, count) in enumerate(zip(stages, counts)):
+        for i, (axes, order) in enumerate(zip(stages, orders)):
             mine[i] = total
             copies = []
-            for step in range(1, count + 1):
+            for step in order:
                 copy = pltpu.make_async_remote_copy(
                     src_ref=mine.at[i],
                     dst_ref=landing[i].at[step - 1],
@@ -383,19 +458,47 @@
             total = total + jnp.sum(landing[i][...], axis=0)
             for copy in copies:
                 copy.wait_send()
-        gram_ref[...] = total[:S, :S] / cells_all
+        gram_ref[...] = total
+
+    def finish_kernel(resp_ref, total_ref, out_ref, gram_ref, sem):
+        copy = pltpu.make_async_copy(resp_ref, out_ref, sem)
+        copy.start()
+        gram_ref[...] = total_ref[:S, :S] / cells_all
+        copy.wait()
+
+    def finish(response, total):
+        return pl.pallas_call(
+            finish_kernel,
+            out_shape=(
+                jax.ShapeDtypeStruct(response.shape, response.dtype),
+                jax.ShapeDtypeStruct((S, S), jnp.float32),
+            ),
+            in_specs=[
+                pl.BlockSpec(memory_space=pl.ANY),
+                pl.BlockSpec(memory_space=pltpu.VMEM),
+            ],
+            out_specs=(
+                pl.BlockSpec(memory_space=pltpu.HBM),
+                pl.BlockSpec(memory_space=pltpu.VMEM),
+            ),
+            scratch_shapes=[pltpu.SemaphoreType.DMA],
+            compiler_params=pltpu.CompilerParams(vmem_limit_bytes=4 << 20),
+            name="finish",
+        )(response, total)
 
     def gram_sum(part):
         f32 = jnp.float32
         return pl.pallas_call(
             gram_kernel,
-            out_shape=jax.ShapeDtypeStruct((S, S), f32),
+            out_shape=pltpu.VMEM((C, 128), f32),
             in_specs=[pl.BlockSpec(memory_space=pltpu.VMEM)],
             out_specs=pl.BlockSpec(memory_space=pltpu.VMEM),
             scratch_shapes=[pltpu.VMEM((2, C, 128), f32)]
             + [pltpu.VMEM((count, C, 128), f32) for count in counts]
             + [pltpu.SemaphoreType.DMA((count,)) for count in counts] * 2,
-            compiler_params=pltpu.CompilerParams(collective_id=1, has_side_effects=True),
+            compiler_params=pltpu.CompilerParams(
+                collective_id=1, has_side_effects=True, vmem_limit_bytes=4 << 20
+            ),
             name="gram_sum",
         )(part)
 
@@ -409,7 +512,8 @@
             harm_lo,
             couple_flags,
         )
-        return response.reshape(shape), gram_sum(part)
+        response, gram_matrix = finish(response, gram_sum(part))
+        return response.reshape(shape), gram_matrix
 
     return jax.shard_map(
         local,

time: 54.4 us -> 49 us (0.901)
  local copies, waits for them, and re-layouts: 2.65 us -> 0 us
  Pallas kernels: 50.2 us -> 47.6 us
    pallas_call x2 -> x3, Pallas kernels: 50.2 us -> 47.6 us  [the longest x1 23.3 us: apply_operator(): pl.pallas_call(halo_kernel, out_shape=(pltpu.VMEM((S, ROWS, N), bf16), pl...]
    unnamed x4 -> x0, local copies, waits for them, and re-layouts: 2.65 us -> none
where the time goes in v2:
time: 49 us; the launch traced here: 48.9 us
  Pallas kernels  47.6 us (97%)
  between operations  1.29 us (3%)
    pallas_call x1, Pallas kernels, apply_operator(): pl.pallas_call(halo_kernel, out_shape=(pltpu.VMEM((S, ROWS, N), bf16), pl...  23.3 us
    pallas_call x1, Pallas kernels, gram_sum(): pl.pallas_call(gram_kernel, out_shape=pltpu.VMEM((C, 128), f32), in_specs...  22.8 us
    pallas_call x1, Pallas kernels, finish(): pl.pallas_call(finish_kernel, out_shape=(jax.ShapeDtypeStruct(response.sh...  1.47 us

profile of v2, /device:TPU:1, one launch (start us, length us, event | category | flops | bytes accessed | tf_op | source)
XLA Modules:
  0.0 48.9 jit_solution(10669358223695839990)
XLA Ops:
  1.3 23.3 %operator.1 = (bf16[4,64,1536]{2,1,0:T(8,128)(2,1)S(1)}, f32[8,128]{1,0:T(8,128)S(1)}) custom-call(bf16[4,64,1536]{2,1,0:T(8,128)(2,1)} %bitcast.6, bf16[4,8,8,1536]{3,2,1,0:T(8,128)(2,1)} %bitcast.7, f32[7,2,1,1536]{3,2,1,0:T(1,128)} %base_ref.1, f32[1536]{0:T(1024)} %mean_ref.1, f32[4,4,7]{2,1,0:T(4,128)} %bitcast.8, s32[1]{0:T(128)S(6)} %copy.9.lo_hbm, ...), custom_call_target="tpu_custom_call" | custom-call | tf_op jit(solution)/shard_map/operator/pallas_call | solution.py:353
  24.6 22.8 %gram_sum.1.total_ref = f32[8,128]{1,0:T(8,128)S(1)} custom-call(f32[8,128]{1,0:T(8,128)S(1)} %get-tuple-element.7.part_ref), custom_call_target="tpu_custom_call" | custom-call | tf_op jit(solution)/shard_map/gram_sum/pallas_call | solution.py:491
  47.4 1.5 %finish.1 = (bf16[4,64,1536]{2,1,0:T(8,128)(2,1)}, f32[4,4]{1,0:T(4,128)}) custom-call(bf16[4,64,1536]{2,1,0:T(8,128)(2,1)S(1)} %get-tuple-element.6.resp_ref, f32[8,128]{1,0:T(8,128)S(1)} %gram_sum.1.total_ref), custom_call_target="tpu_custom_call" | custom-call | tf_op jit(solution)/shard_map/finish/pallas_call | solution.py:470

commit v3 on v2

--- a/solution.py
+++ b/solution.py
@@ -17,7 +17,7 @@
 CROWS = ROWS // CHUNKS
 RIM = 3 * C
 Y = 4
-DIRECT = 2
+DIRECT = 1
 LANES = 256
 
 OWN = [(j, k, k - j + 3) for k in range(K) for j in range(7) if 0 <= k - j + 3 < K]
@@ -165,6 +165,18 @@
 
     start_planes(range(CHUNKS // 2))
 
+    @when(middle, hop)
+    def _():
+        to_relay(0).wait_recv()
+
+    for way, far in ((0, up_hop), (1, down_hop)):
+
+        @when(middle, far)
+        def _():
+            from_relay(way).start()
+
+    start_planes(range(CHUNKS // 2, CHUNKS))
+
     for way, there in ((0, has_d), (1, has_u)):
 
         @pl.when(jnp.logical_not(there))
@@ -200,18 +212,6 @@
     for j in range(7):
         re_ref[j] = jnp.broadcast_to(base_in[j, 0], (C, N))
         im_ref[j] = jnp.broadcast_to(base_in[j, 1], (C, N))
-
-    @when(middle, hop)
-    def _():
-        to_relay(0).wait_recv()
-
-    for way, far in ((0, up_hop), (1, down_hop)):
-
-        @when(middle, far)
-        def _():
-            from_relay(way).start()
-
-    start_planes(range(CHUNKS // 2, CHUNKS))
 
     own_high, own_low = split(own_coeff[...])
     own_both = jnp.concatenate([own_high, own_low], axis=1)
@@ -460,11 +460,17 @@
                 copy.wait_send()
         gram_ref[...] = total
 
-    def finish_kernel(resp_ref, total_ref, out_ref, gram_ref, sem):
-        copy = pltpu.make_async_copy(resp_ref, out_ref, sem)
-        copy.start()
-        gram_ref[...] = total_ref[:S, :S] / cells_all
-        copy.wait()
+    def finish_kernel(resp_ref, total_ref, out_ref, gram_ref, gram_here, sem):
+        copies = [
+            pltpu.make_async_copy(resp_ref.at[s], out_ref.at[s], sem.at[s]) for s in range(S)
+        ]
+        for copy in copies:
+            copy.start()
+        gram_here[...] = total_ref[:S, :S] / cells_all
+        copies.append(pltpu.make_async_copy(gram_here, gram_ref, sem.at[S]))
+        copies[S].start()
+        for copy in copies:
+            copy.wait()
 
     def finish(response, total):
         return pl.pallas_call(
@@ -479,9 +485,12 @@
             ],
             out_specs=(
                 pl.BlockSpec(memory_space=pltpu.HBM),
-                pl.BlockSpec(memory_space=pltpu.VMEM),
+                pl.BlockSpec(memory_space=pltpu.HBM),
             ),
-            scratch_shapes=[pltpu.SemaphoreType.DMA],
+            scratch_shapes=[
+                pltpu.VMEM((S, S), jnp.float32),
+                pltpu.SemaphoreType.DMA((S + 1,)),
+            ],
             compiler_params=pltpu.CompilerParams(vmem_limit_bytes=4 << 20),
             name="finish",
         )(response, total)

time: 49 us -> 47.2 us (0.963)
  Pallas kernels: 47.6 us -> 45.8 us
    pallas_call x1, Pallas kernels: 22.8 us -> 20.5 us  [gram_sum(): pl.pallas_call(gram_kernel, out_shape=pltpu.VMEM((C, 128), f32), in_specs...]
    pallas_call x1, Pallas kernels: 23.3 us -> 24.4 us  [apply_operator(): pl.pallas_call(halo_kernel, out_shape=(pltpu.VMEM((S, ROWS, N), bf16), pl...]
    pallas_call x1, Pallas kernels: 1.47 us -> 0.92 us  [finish(): pl.pallas_call(finish_kernel, out_shape=(jax.ShapeDtypeStruct(response.sh...]
where the time goes in v3:
time: 47.2 us; the launch traced here: 47.1 us
  Pallas kernels  45.8 us (97%)
  between operations  1.29 us (3%)
    pallas_call x1, Pallas kernels, apply_operator(): pl.pallas_call(halo_kernel, out_shape=(pltpu.VMEM((S, ROWS, N), bf16), pl...  24.4 us
    pallas_call x1, Pallas kernels, gram_sum(): pl.pallas_call(gram_kernel, out_shape=pltpu.VMEM((C, 128), f32), in_specs...  20.5 us

profile of v3, /device:TPU:1, one launch (start us, length us, event | category | flops | bytes accessed | tf_op | source)
XLA Modules:
  0.0 47.1 jit_solution(6313198043243499289)
XLA Ops:
  1.3 24.4 %operator.1 = (bf16[4,64,1536]{2,1,0:T(8,128)(2,1)S(1)}, f32[8,128]{1,0:T(8,128)S(1)}) custom-call(bf16[4,64,1536]{2,1,0:T(8,128)(2,1)} %bitcast.6, bf16[4,8,8,1536]{3,2,1,0:T(8,128)(2,1)} %bitcast.7, f32[7,2,1,1536]{3,2,1,0:T(1,128)} %base_ref.1, f32[1536]{0:T(1024)} %mean_ref.1, f32[4,4,7]{2,1,0:T(4,128)} %bitcast.8, s32[1]{0:T(128)S(6)} %copy.9.lo_hbm, ...), custom_call_target="tpu_custom_call" | custom-call | tf_op jit(solution)/shard_map/operator/pallas_call | solution.py:353
  25.7 20.5 %gram_sum.1.total_ref = f32[8,128]{1,0:T(8,128)S(1)} custom-call(f32[8,128]{1,0:T(8,128)S(1)} %get-tuple-element.7.part_ref), custom_call_target="tpu_custom_call" | custom-call | tf_op jit(solution)/shard_map/gram_sum/pallas_call | solution.py:500
  46.1 0.9 %finish.1 = (bf16[4,64,1536]{2,1,0:T(8,128)(2,1)}, f32[4,4]{1,0:T(4,128)}) custom-call(bf16[4,64,1536]{2,1,0:T(8,128)(2,1)S(1)} %get-tuple-element.6.resp_ref, f32[8,128]{1,0:T(8,128)S(1)} %gram_sum.1.total_ref), custom_call_target="tpu_custom_call" | custom-call | tf_op jit(solution)/shard_map/finish/pallas_call | solution.py:476

commit v4 on v3

--- a/solution.py
+++ b/solution.py
@@ -315,12 +315,17 @@
         for p in range(len(PAIRS)):
             gram_ref[p] = sums[p]
 
-    row, col = pair_iota(128)
-    tile = jnp.zeros((C, 128), jnp.float32)
+    row = lax.broadcasted_iota(jnp.int32, (2 * C, 128), 0)
+    col = lax.broadcasted_iota(jnp.int32, (2 * C, 128), 1)
+    stacked = jnp.zeros((2 * C, 128), jnp.float32)
+    hit = row < 0
     for p, (s, t) in enumerate(PAIRS):
-        total = jnp.sum(gram_ref[p])
-        hit = ((row == s) & (col == t)) | ((row == t) & (col == s))
-        tile = jnp.where(hit, total, tile)
+        folded = gram_ref[p][:, :128] + gram_ref[p][:, 128:]
+        total = jnp.sum(folded, axis=0, keepdims=True)
+        stacked = jnp.where(row == p, total, stacked)
+        hit = hit | ((row == p) & ((col == S * s + t) | (col == S * t + s)))
+    sums = jnp.sum(stacked, axis=1, keepdims=True)
+    tile = jnp.sum(jnp.where(hit, sums, 0.0), axis=0, keepdims=True)
     part_ref[...] = tile
 
     for part in range(CHUNKS):
@@ -354,7 +359,7 @@
         halo_kernel,
         out_shape=(
             pltpu.VMEM((S, ROWS, N), bf16),
-            pltpu.VMEM((C, 128), f32),
+            pltpu.VMEM((1, 128), f32),
         ),
         in_specs=[hbm] * 7,
         out_specs=(vmem, vmem),
@@ -397,7 +402,7 @@
     y, xh, core, xl = 4, 2, 2, 2
     z = n_space // (xh * y)
     sizes = {"z": z, "xh": xh, "y": y, "xl": xl, "core": core}
-    stages = [("z", "core"), ("xh", "xl", "y")]
+    stages = [("xh", "xl", "core"), ("z", "y")]
     counts, orders = [], []
 
     def hops(axes, step):
@@ -439,6 +444,7 @@
                 )
         pl.semaphore_wait(barrier, sum(counts))
         total = part_ref[...]
+        sent = []
         for i, (axes, order) in enumerate(zip(stages, orders)):
             mine[i] = total
             copies = []
@@ -456,9 +462,10 @@
             for copy in copies:
                 copy.wait_recv()
             total = total + jnp.sum(landing[i][...], axis=0)
-            for copy in copies:
-                copy.wait_send()
+            sent += copies
         gram_ref[...] = total
+        for copy in sent:
+            copy.wait_send()
 
     def finish_kernel(resp_ref, total_ref, out_ref, gram_ref, gram_here, sem):
         copies = [
@@ -466,7 +473,12 @@
         ]
         for copy in copies:
             copy.start()
-        gram_here[...] = total_ref[:S, :S] / cells_all
+        total = total_ref[...] / cells_all
+        row, _col = pair_iota(128)
+        tile = jnp.broadcast_to(total, (C, 128))
+        for s in range(1, S):
+            tile = jnp.where(row == s, pltpu.roll(total, 128 - S * s, 1), tile)
+        gram_here[...] = tile[:S, :S]
         copies.append(pltpu.make_async_copy(gram_here, gram_ref, sem.at[S]))
         copies[S].start()
         for copy in copies:
@@ -499,11 +511,11 @@
         f32 = jnp.float32
         return pl.pallas_call(
             gram_kernel,
-            out_shape=pltpu.VMEM((C, 128), f32),
+            out_shape=pltpu.VMEM((1, 128), f32),
             in_specs=[pl.BlockSpec(memory_space=pltpu.VMEM)],
             out_specs=pl.BlockSpec(memory_space=pltpu.VMEM),
-            scratch_shapes=[pltpu.VMEM((2, C, 128), f32)]
-            + [pltpu.VMEM((count, C, 128), f32) for count in counts]
+            scratch_shapes=[pltpu.VMEM((2, 1, 128), f32)]
+            + [pltpu.VMEM((count, 1, 128), f32) for count in counts]
             + [pltpu.SemaphoreType.DMA((count,)) for count in counts] * 2,
             compiler_params=pltpu.CompilerParams(
                 collective_id=1, has_side_effects=True, vmem_limit_bytes=4 << 20

time: 47.2 us -> 46.5 us (0.985)
  Pallas kernels: 45.8 us -> 45.1 us
    pallas_call x1, Pallas kernels: 20.5 us -> 19.8 us  [gram_sum(): pl.pallas_call(gram_kernel, out_shape=pltpu.VMEM((1, 128), f32), in_specs...]
where the time goes in v4:
time: 46.5 us; the launch traced here: 46.3 us
  Pallas kernels  45.1 us (97%)
  between operations  1.29 us (3%)
    pallas_call x1, Pallas kernels, apply_operator(): pl.pallas_call(halo_kernel, out_shape=(pltpu.VMEM((S, ROWS, N), bf16), pl...  24.4 us
    pallas_call x1, Pallas kernels, gram_sum(): pl.pallas_call(gram_kernel, out_shape=pltpu.VMEM((1, 128), f32), in_specs...  19.8 us

profile of v4, /device:TPU:1, one launch (start us, length us, event | category | flops | bytes accessed | tf_op | source)
XLA Modules:
  0.0 46.3 jit_solution(11175345267697986803)
XLA Ops:
  1.3 24.4 %operator.1 = (bf16[4,64,1536]{2,1,0:T(8,128)(2,1)S(1)}, f32[1,128]{1,0:T(1,128)S(1)}) custom-call(bf16[4,64,1536]{2,1,0:T(8,128)(2,1)} %bitcast.6, bf16[4,8,8,1536]{3,2,1,0:T(8,128)(2,1)} %bitcast.7, f32[7,2,1,1536]{3,2,1,0:T(1,128)} %base_ref.1, f32[1536]{0:T(1024)} %mean_ref.1, f32[4,4,7]{2,1,0:T(4,128)} %bitcast.8, s32[1]{0:T(128)S(6)} %copy.9.lo_hbm, ...), custom_call_target="tpu_custom_call" | custom-call | tf_op jit(solution)/shard_map/operator/pallas_call | solution.py:358
  25.6 19.8 %gram_sum.1.total_ref = f32[1,128]{1,0:T(1,128)S(1)} custom-call(f32[1,128]{1,0:T(1,128)S(1)} %get-tuple-element.7.part_ref), custom_call_target="tpu_custom_call" | custom-call | tf_op jit(solution)/shard_map/gram_sum/pallas_call | solution.py:512
  45.4 0.9 %finish.1 = (bf16[4,64,1536]{2,1,0:T(8,128)(2,1)}, f32[4,4]{1,0:T(4,128)}) custom-call(bf16[4,64,1536]{2,1,0:T(8,128)(2,1)S(1)} %get-tuple-element.6.resp_ref, f32[1,128]{1,0:T(1,128)S(1)} %gram_sum.1.total_ref), custom_call_target="tpu_custom_call" | custom-call | tf_op jit(solution)/shard_map/finish/pallas_call | solution.py:488

commit v5 on v4

--- a/solution.py
+++ b/solution.py
@@ -253,7 +253,7 @@
 
     lax.fori_loop(0, S, local_part, 0)
 
-    for way, there, far, listed in ((0, has_d, down_hop, LEFT), (1, has_u, up_hop, RIGHT)):
+    def add_rim(way, there, far, listed):
         split_up = jnp.logical_and(edge, far)
 
         @when(there, jnp.logical_not(split_up))
@@ -288,7 +288,8 @@
 
     gram_ref[...] = jnp.zeros_like(gram_ref)
     half = 0.5 * mean_in[...].reshape(1, N)
-    for part in range(CHUNKS):
+
+    def finish_part(part):
         rows = slice(part * CROWS, (part + 1) * CROWS)
         for way, there in ((0, has_l), (1, has_r)):
 
@@ -314,6 +315,11 @@
                 sums[p] = sums[p] + (product[:C] + product[C:])
         for p in range(len(PAIRS)):
             gram_ref[p] = sums[p]
+
+    for way, there, far, listed in ((0, has_d, down_hop, LEFT), (1, has_u, up_hop, RIGHT)):
+        add_rim(way, there, far, listed)
+        for part in range(way * (CHUNKS // 2), (way + 1) * (CHUNKS // 2)):
+            finish_part(part)
 
     row = lax.broadcasted_iota(jnp.int32, (2 * C, 128), 0)
     col = lax.broadcasted_iota(jnp.int32, (2 * C, 128), 1)

time: 46.5 us -> 46.5 us (level)
  no operation moved by 1% of the time
where the time goes in v5:
time: 46.5 us; the launch traced here: 46.3 us
  Pallas kernels  45.1 us (97%)
  between operations  1.29 us (3%)
    pallas_call x1, Pallas kernels, apply_operator(): pl.pallas_call(halo_kernel, out_shape=(pltpu.VMEM((S, ROWS, N), bf16), pl...  24.4 us
    pallas_call x1, Pallas kernels, gram_sum(): pl.pallas_call(gram_kernel, out_shape=pltpu.VMEM((1, 128), f32), in_specs...  19.8 us

profile of v5, /device:TPU:1, one launch (start us, length us, event | category | flops | bytes accessed | tf_op | source)
XLA Modules:
  0.0 46.3 jit_solution(2874861428819138382)
XLA Ops:
  1.3 24.4 %operator.1 = (bf16[4,64,1536]{2,1,0:T(8,128)(2,1)S(1)}, f32[1,128]{1,0:T(1,128)S(1)}) custom-call(bf16[4,64,1536]{2,1,0:T(8,128)(2,1)} %bitcast.6, bf16[4,8,8,1536]{3,2,1,0:T(8,128)(2,1)} %bitcast.7, f32[7,2,1,1536]{3,2,1,0:T(1,128)} %base_ref.1, f32[1536]{0:T(1024)} %mean_ref.1, f32[4,4,7]{2,1,0:T(4,128)} %bitcast.8, s32[1]{0:T(128)S(6)} %copy.9.lo_hbm, ...), custom_call_target="tpu_custom_call" | custom-call | tf_op jit(solution)/shard_map/operator/pallas_call | solution.py:364
  25.6 19.8 %gram_sum.1.total_ref = f32[1,128]{1,0:T(1,128)S(1)} custom-call(f32[1,128]{1,0:T(1,128)S(1)} %get-tuple-element.7.part_ref), custom_call_target="tpu_custom_call" | custom-call | tf_op jit(solution)/shard_map/gram_sum/pallas_call | solution.py:518
  45.4 0.9 %finish.1 = (bf16[4,64,1536]{2,1,0:T(8,128)(2,1)}, f32[4,4]{1,0:T(4,128)}) custom-call(bf16[4,64,1536]{2,1,0:T(8,128)(2,1)S(1)} %get-tuple-element.6.resp_ref, f32[1,128]{1,0:T(1,128)S(1)} %gram_sum.1.total_ref), custom_call_target="tpu_custom_call" | custom-call | tf_op jit(solution)/shard_map/finish/pallas_call | solution.py:494

commit v6 on v5

--- a/solution.py
+++ b/solution.py
@@ -408,7 +408,7 @@
     y, xh, core, xl = 4, 2, 2, 2
     z = n_space // (xh * y)
     sizes = {"z": z, "xh": xh, "y": y, "xl": xl, "core": core}
-    stages = [("xh", "xl", "core"), ("z", "y")]
+    stages = [("z", "y"), ("xh", "xl", "core")]
     counts, orders = [], []
 
     def hops(axes, step):

time: 46.5 us -> 47.3 us (1.017)
  Pallas kernels: 45.1 us -> 45.9 us
    pallas_call x1, Pallas kernels: 19.8 us -> 20.6 us  [gram_sum(): pl.pallas_call(gram_kernel, out_shape=pltpu.VMEM((1, 128), f32), in_specs...]
where the time goes in v6:
time: 47.3 us; the launch traced here: 47.1 us
  Pallas kernels  45.9 us (97%)
  between operations  1.29 us (3%)
    pallas_call x1, Pallas kernels, apply_operator(): pl.pallas_call(halo_kernel, out_shape=(pltpu.VMEM((S, ROWS, N), bf16), pl...  24.4 us
    pallas_call x1, Pallas kernels, gram_sum(): pl.pallas_call(gram_kernel, out_shape=pltpu.VMEM((1, 128), f32), in_specs...  20.6 us

profile of v6, /device:TPU:1, one launch (start us, length us, event | category | flops | bytes accessed | tf_op | source)
XLA Modules:
  0.0 47.1 jit_solution(1622195437733820388)
XLA Ops:
  1.3 24.4 %operator.1 = (bf16[4,64,1536]{2,1,0:T(8,128)(2,1)S(1)}, f32[1,128]{1,0:T(1,128)S(1)}) custom-call(bf16[4,64,1536]{2,1,0:T(8,128)(2,1)} %bitcast.6, bf16[4,8,8,1536]{3,2,1,0:T(8,128)(2,1)} %bitcast.7, f32[7,2,1,1536]{3,2,1,0:T(1,128)} %base_ref.1, f32[1536]{0:T(1024)} %mean_ref.1, f32[4,4,7]{2,1,0:T(4,128)} %bitcast.8, s32[1]{0:T(128)S(6)} %copy.9.lo_hbm, ...), custom_call_target="tpu_custom_call" | custom-call | tf_op jit(solution)/shard_map/operator/pallas_call | solution.py:364
  25.6 20.6 %gram_sum.1.total_ref = f32[1,128]{1,0:T(1,128)S(1)} custom-call(f32[1,128]{1,0:T(1,128)S(1)} %get-tuple-element.7.part_ref), custom_call_target="tpu_custom_call" | custom-call | tf_op jit(solution)/shard_map/gram_sum/pallas_call | solution.py:518
  46.2 0.9 %finish.1 = (bf16[4,64,1536]{2,1,0:T(8,128)(2,1)}, f32[4,4]{1,0:T(4,128)}) custom-call(bf16[4,64,1536]{2,1,0:T(8,128)(2,1)S(1)} %get-tuple-element.6.resp_ref, f32[1,128]{1,0:T(1,128)S(1)} %gram_sum.1.total_ref), custom_call_target="tpu_custom_call" | custom-call | tf_op jit(solution)/shard_map/finish/pallas_call | solution.py:494

commit v7 on v5

--- a/solution.py
+++ b/solution.py
@@ -89,8 +89,6 @@
         ((mix_hbm, mix_ref), (lo_hbm, lo_ref), (flag_hbm, flag_ref))
     ):
         loads.append(pltpu.make_async_copy(source, target, in_sem.at[3 + i]))
-    for load in loads:
-        load.start()
     peers = sum(there.astype(jnp.int32) for there, _ in greeted)
     pl.semaphore_wait(barrier, peers)
 
@@ -164,6 +162,8 @@
                     plane_copy(way, part).start()
 
     start_planes(range(CHUNKS // 2))
+    for load in loads:
+        load.start()
 
     @when(middle, hop)
     def _():

time: 46.5 us -> 46.5 us (level)
  no operation moved by 1% of the time
where the time goes in v7:
time: 46.5 us; the launch traced here: 46.3 us
  Pallas kernels  45.1 us (97%)
  between operations  1.29 us (3%)
    pallas_call x1, Pallas kernels, apply_operator(): pl.pallas_call(halo_kernel, out_shape=(pltpu.VMEM((S, ROWS, N), bf16), pl...  24.4 us
    pallas_call x1, Pallas kernels, gram_sum(): pl.pallas_call(gram_kernel, out_shape=pltpu.VMEM((1, 128), f32), in_specs...  19.8 us

profile of v7, /device:TPU:1, one launch (start us, length us, event | category | flops | bytes accessed | tf_op | source)
XLA Modules:
  0.0 46.3 jit_solution(3492198365066886941)
XLA Ops:
  1.3 24.4 %operator.1 = (bf16[4,64,1536]{2,1,0:T(8,128)(2,1)S(1)}, f32[1,128]{1,0:T(1,128)S(1)}) custom-call(bf16[4,64,1536]{2,1,0:T(8,128)(2,1)} %bitcast.6, bf16[4,8,8,1536]{3,2,1,0:T(8,128)(2,1)} %bitcast.7, f32[7,2,1,1536]{3,2,1,0:T(1,128)} %base_ref.1, f32[1536]{0:T(1024)} %mean_ref.1, f32[4,4,7]{2,1,0:T(4,128)} %bitcast.8, s32[1]{0:T(128)S(6)} %copy.9.lo_hbm, ...), custom_call_target="tpu_custom_call" | custom-call | tf_op jit(solution)/shard_map/operator/pallas_call | solution.py:364
  25.6 19.8 %gram_sum.1.total_ref = f32[1,128]{1,0:T(1,128)S(1)} custom-call(f32[1,128]{1,0:T(1,128)S(1)} %get-tuple-element.7.part_ref), custom_call_target="tpu_custom_call" | custom-call | tf_op jit(solution)/shard_map/gram_sum/pallas_call | solution.py:518
  45.4 0.9 %finish.1 = (bf16[4,64,1536]{2,1,0:T(8,128)(2,1)}, f32[4,4]{1,0:T(4,128)}) custom-call(bf16[4,64,1536]{2,1,0:T(8,128)(2,1)S(1)} %get-tuple-element.6.resp_ref, f32[1,128]{1,0:T(1,128)S(1)} %gram_sum.1.total_ref), custom_call_target="tpu_custom_call" | custom-call | tf_op jit(solution)/shard_map/finish/pallas_call | solution.py:494
